TPU v7x, 256 devices: a whole 4x4x8 slice. The times are simulated.
256 devices in a mesh: mod: 8 (over z), dp: 32 (over x, y, core).
Axes of the slice: x: 4, y: 4, z: 8, core: 2. Of those that a mesh axis runs over, the one named last changes fastest.
Arguments:
- train_grads: float32 [4096, 128, 512], P('dp', 'mod'), may hold values from -50 to 50
- queries: float32 [128, 128, 512], P('dp', 'mod'), may hold values from -6 to 6
- damping: float32 [128], P('mod'), may hold values from 0.05 to 0.5
Outputs:
- scores: float32 [4096, 128], P('dp', 'mod')
All inputs are finite; a program needn't handle non-finite values.
Results may differ from a plain program's by a relative error of at most 0.012.
Values sent between devices are 32-bit elements; how exact they have to be, the bound alone decides.
A program may use at most 128 MiB of HBM per device.

v0:
```python
import math

import jax
import jax.numpy as jnp
from jax import lax
from jax.sharding import PartitionSpec as P

NEWTON_STEPS = 8


epsilon = 1e-06


def partner_2(value, axis, stride):
    return lax.ppermute(value, axis, [(i, i ^ 1 << stride) for i in range(lax.axis_size(axis))])


def join_halves(mine, theirs, pair_side):
    return jnp.where(
        pair_side == 0, jnp.concatenate([mine, theirs], 0), jnp.concatenate([theirs, mine], 0)
    )


def per_device(train_grads, queries, damping):
    highest = lax.Precision.HIGHEST
    rows_dev, group_mods, width = train_grads.shape
    half_width = width // 2
    dp_count = lax.axis_size("dp")
    mod_count = lax.axis_size("mod")
    total_rows = rows_dev * dp_count
    dp_index = lax.axis_index("dp")
    pair_side = dp_index % 2
    owned_module = dp_index // 2
    paired = train_grads.reshape(rows_dev, group_mods * 2, half_width)
    pieces = half_width * lax.axis_size("dp") // half_width
    picked = jnp.arange(pieces, dtype=jnp.int32)
    left_cols = jnp.take(paired, picked, axis=1)
    right_cols = jnp.take(train_grads, picked // 2, axis=1)
    outer_sum = jnp.einsum(
        "rpa,rpb->pab", left_cols, right_cols, precision=highest, preferred_element_type=jnp.float32
    )
    own_rows = lax.psum_scatter(
        (outer_sum / total_rows).reshape(half_width * lax.axis_size("dp"), width),
        "dp",
        scatter_dimension=0,
        tiled=True,
    )
    damp_value = lax.dynamic_slice_in_dim(damping, owned_module, 1, 0)[0]
    identity_mat = jnp.eye(width, dtype=jnp.float32)
    partner = partner_2(own_rows, "dp", 0)
    fisher = join_halves(own_rows, partner, pair_side)
    trace_all = jnp.trace(fisher)
    damp_shift = damp_value * trace_all / width
    system = fisher + damp_shift * identity_mat
    frob_norm = jnp.sqrt(jnp.sum(system * system) + epsilon)
    inverse = identity_mat / frob_norm
    for iteration in range(NEWTON_STEPS):
        product = jnp.dot(
            jnp.dot(inverse, system, precision=highest, preferred_element_type=jnp.float32),
            inverse,
            precision=highest,
            preferred_element_type=jnp.float32,
        )
        inverse = 2.0 * inverse - product
    query_dev = queries.shape[0]
    query_half = query_dev // 2
    outgoing = (
        queries.reshape(2, query_half, group_mods, width)
        .transpose(2, 0, 1, 3)
        .reshape(group_mods * 2, query_half, width)
    )
    arrived_queries = lax.all_to_all(outgoing, "dp", split_axis=0, concat_axis=1, tiled=True)[0]
    conditioned = jnp.dot(
        arrived_queries, inverse, precision=highest, preferred_element_type=jnp.float32
    )
    scale_factor = math.sqrt(group_mods * mod_count * width)
    shard_piece = lax.all_gather(conditioned[None], "dp", axis=0, tiled=True)
    pieces = shard_piece.shape[0]
    owners = jnp.arange(pieces, dtype=jnp.int32)
    chosen = jnp.take(train_grads, owners // 2, axis=1)
    inner = jnp.einsum(
        "rnk,njk->rnj", chosen, shard_piece, precision=highest, preferred_element_type=jnp.float32
    )
    inner = inner.reshape(rows_dev, pieces, dp_count, query_half)
    selector = (owners[:, None] % 2 == jnp.arange(2, dtype=jnp.int32)[None, :]).astype(jnp.float32)
    summed = jnp.einsum(
        "rnis,nh->rihs", inner, selector, precision=highest, preferred_element_type=jnp.float32
    )
    partial_value = summed.reshape(rows_dev, dp_count * query_dev) / scale_factor
    return lax.psum_scatter(partial_value, "mod", scatter_dimension=1, tiled=True)


def solution(mesh):
    return jax.shard_map(
        per_device,
        mesh=mesh,
        in_specs=(P("dp", "mod", None), P("dp", "mod", None), P("mod")),
        out_specs=P("dp", "mod"),
        check_vma=False,
    )
```

profile of v0, /device:TPU:2, one launch (start us, length us, event | category | flops | bytes accessed | tf_op | source)
XLA Modules:
  0.0 361.1 jit_solution(18099335862455351523)
XLA Ops:
  6.5 0.0 reduce-scatter.3.cloned.1.call-start
  6.6 5.4 %copy.13 = f32[128,16,512]{0,2,1:T(8,128)} copy(f32[128,16,512]{2,1,0:T(8,128)} %param.5) | data formatting | bytes 8388608 | tf_op args[0]
  11.9 13.2 %gather_fusion.1 = f32[32,128,512]{2,0,1:T(8,128)} fusion(f32[128,16,512]{2,1,0:T(8,128)} %param.5, s32[1024]{0:T(1024)S(1)} %pad_clamp_fusion), kind=kCustom, calls=%fused_computation.clone | custom fusion | bytes 16777344 | tf_op jit(solution)/shard_map/jit(_take)/gather | solution.py:38
  25.1 5.6 %copy.14 = f32[128,32,256]{2,0,1:T(8,128)} copy(f32[128,32,256]{0,2,1:T(8,128)} %bitcast.52) | data formatting | bytes 8388608 | tf_op jit(solution)/shard_map/reshape | solution.py:34
  30.7 8.6 %select_bitcast_fusion = f32[128,32,512]{2,1,0:T(8,128)} fusion(f32[32,128,512]{2,0,1:T(8,128)} %gather_fusion.1, pred[32]{0:T(512)(128)(4,1)S(1)} %compare_and_fusion), kind=kLoop, calls=%fused_computation.3 | loop fusion | flops 2097152 | bytes 16777248 | tf_op jit(solution)/shard_map/jit(_take)/select_n | solution.py:38
  39.4 4.9 %gather_fusion = f32[32,128,256]{2,1,0:T(8,128)} fusion(f32[128,32,256]{2,0,1:T(8,128)} %copy.14, s32[1024]{0:T(1024)S(1)} %pad_clamp_fusion.1), kind=kCustom, calls=%fused_computation.1 | custom fusion | bytes 8388736 | tf_op jit(solution)/shard_map/jit(_take)/gather | solution.py:37
  44.3 26.7 %convolution_multiply_fusion = f32[32,256,512]{2,1,0:T(8,128)} fusion(f32[128,32,512]{2,1,0:T(8,128)} %select_bitcast_fusion, f32[32,128,256]{2,1,0:T(8,128)} %gather_fusion, pred[32]{0:T(512)(128)(4,1)S(1)} %iota_compare_fusion.3), kind=kOutput, calls=%fused_computation.2 | convolution fusion | flops 6447693824 | bytes 29360160 | tf_op jit(solution)/shard_map/rpa,rpb->pab/dot_general | solution.py:39
  71.0 0.0 copy-start.1
  71.0 0.0 reduce-scatter.3.cloned.1.call-update
  71.0 125.9 %reduce-scatter.3.cloned.1.call-done = f32[256,512]{1,0:T(8,128)} async-done(((f32[8192,512]{1,0:T(8,128)}), f32[256,512]{1,0:T(8,128)}) %reduce-scatter.3.cloned.1.call-update) | async-done | bytes 524304 | tf_op jit(solution)/shard_map/reduce_scatter | solution.py:42
  196.9 0.0 collective-permute-start
  196.9 0.0 copy-done.1
  196.9 0.7 copy.17
  197.7 5.7 %all-to-all-start = ((f32[32,2,512]{2,1,0:T(2,128)}), f32[32,2,512]{2,1,0:T(2,128)S(1)}, u32[]{:S(2)}, u32[]{:S(2)}) async-start(f32[32,2,512]{2,1,0:T(2,128)} %bitcast.9), calls=%async_computation.1 | async-start | bytes 262144 | tf_op jit(solution)/shard_map/all_to_all | solution.py:72
  203.4 0.2 all-gather.3.cloned.1.call-start
  203.6 0.0 copy-done.2
  203.6 0.6 dynamic_slice.3
  204.2 5.8 %all-to-all-done = f32[32,2,512]{2,1,0:T(2,128)S(1)} async-done(((f32[32,2,512]{2,1,0:T(2,128)}), f32[32,2,512]{2,1,0:T(2,128)S(1)}, u32[]{:S(2)}, u32[]{:S(2)}) %all-to-all-start) | async-done | bytes 131104 | tf_op jit(solution)/shard_map/all_to_all | solution.py:72
  210.0 0.1 squeeze.7
  210.1 0.0 collective-permute-done
  210.1 1.9 select_reduce_fusion
  213.3 2.1 multiply_reduce_fusion
  216.1 3.1 fusion.9
  219.2 1.8 fusion.11
  221.0 0.0 copy-done
  221.0 1.9 fusion.33
  222.9 1.9 convolution_subtract_fusion.6
  224.8 1.9 fusion.32
  226.7 1.9 convolution_subtract_fusion.5
  228.5 2.3 fusion.31
  230.9 1.9 convolution_subtract_fusion.4
  232.7 1.9 fusion.30
  234.6 1.9 convolution_subtract_fusion.3
  236.5 1.9 fusion.29
  238.4 1.9 convolution_subtract_fusion.2
  240.3 1.9 fusion.28
  242.2 2.0 convolution_subtract_fusion.1
  244.2 1.9 fusion.27
  246.2 1.9 convolution_subtract_fusion
  248.0 1.4 convolution_bitcast_fusion
  249.5 0.0 all-gather.3.cloned.1.call-update
  249.5 0.0 reduce-scatter.5.cloned.1.call-start
  249.6 49.6 %all-gather.3.cloned.1.call-done = f32[2048,512]{1,0:T(8,128)} async-done(((f32[64,512]{1,0:T(8,128)}), f32[2048,512]{1,0:T(8,128)}) %all-gather.3.cloned.1.call-update) | async-done | bytes 4194320 | tf_op jit(solution)/shard_map/all_gather | solution.py:77
  299.2 17.2 %fusion = f32[32,64,128]{2,1,0:T(8,128)S(1)} fusion(f32[32,64,512]{2,1,0:T(8,128)} %bitcast.53, f32[128,32,512]{2,1,0:T(8,128)} %select_bitcast_fusion), kind=kOutput, calls=%fused_computation.4 | convolution fusion | flops 1610612736 | bytes 13631488 | tf_op jit(solution)/shard_map/rnk,njk->rnj/dot_general | solution.py:81
  316.4 1.0 fusion.14
  317.4 0.7 copy.20
  318.1 0.0 reduce-scatter.5.cloned.1.call-update
  318.1 36.3 %reduce-scatter.5.cloned.1.call-done = f32[128,16]{0,1:T(8,128)} async-done(((f32[128,128]{0,1:T(8,128)}), f32[128,16]{0,1:T(8,128)}) %reduce-scatter.5.cloned.1.call-update) | async-done | bytes 8208 | tf_op jit(solution)/shard_map/reduce_scatter | solution.py:90
  (9 shorter events, 0.0 us)
Async XLA Ops:
  6.5 190.4 %reduce-scatter.3.cloned.1.call-start = ((), (), s32[]{:S(2)}) async-start(), calls=%async_computation.3 | async-start | bytes 17301504 | tf_op jit(solution)/shard_map/reduce_scatter | solution.py:42
  71.0 125.9 %copy-start.1 = (f32[4,16,512]{2,1,0:T(8,128)S(1)}, f32[4,16,512]{2,1,0:T(8,128)}, u32[]{:S(2)}) copy-start(f32[4,16,512]{2,1,0:T(8,128)} %param.6) | copy-start | bytes 393220
  71.0 132.6 %copy-start.2 = (f32[16]{0:T(128)S(1)}, f32[16]{0:T(128)}, u32[]{:S(2)}) copy-start(f32[16]{0:T(128)} %param.7) | copy-start | bytes 196
  196.9 24.1 %copy-start = (f32[256,512]{1,0:T(8,128)S(1)}, f32[256,512]{1,0:T(8,128)}, u32[]{:S(2)}) copy-start(f32[256,512]{1,0:T(8,128)} %reduce-scatter.3.cloned.1.call-done) | copy-start | bytes 1572868
  196.9 13.2 %collective-permute-start = (f32[256,512]{1,0:T(8,128)}, f32[256,512]{1,0:T(8,128)S(1)}, u32[]{:S(2)}, u32[]{:S(2)}) collective-permute-start(f32[256,512]{1,0:T(8,128)} %reduce-scatter.3.cloned.1.call-done), channel_id=1, source_target_pairs={{0,1},{1,0},{2,3},{3,2},{4,5},{5,4},{6,7},{7,6},{8,9},{9,8},{10,11... | collective-permute-start | bytes 1572872 | tf_op jit(solution)/shard_map/ppermute | solution.py:15
  197.7 12.3 %all-to-all-start = ((f32[32,2,512]{2,1,0:T(2,128)}), f32[32,2,512]{2,1,0:T(2,128)S(1)}, u32[]{:S(2)}, u32[]{:S(2)}) async-start(f32[32,2,512]{2,1,0:T(2,128)} %bitcast.9), calls=%async_computation.1 | async-start | bytes 262144 | tf_op jit(solution)/shard_map/all_to_all | solution.py:72
  203.4 95.8 %all-gather.3.cloned.1.call-start = ((), (), s32[]{:S(2)}) async-start(), calls=%async_computation.5 | async-start | bytes 4325376 | tf_op jit(solution)/shard_map/all_gather | solution.py:77
  249.5 104.9 %reduce-scatter.5.cloned.1.call-start = ((), (), s32[]{:S(2)}) async-start(), calls=%async_computation.4 | async-start | bytes 73728 | tf_op jit(solution)/shard_map/reduce_scatter | solution.py:90
Sparse Core Ops, SparseCore 0:
  71.2 125.7 reduce-scatter.2
  249.6 49.4 all-gather.2
  318.2 36.1 reduce-scatter.4
where the time goes:
time: 368 us; the launch traced here: 361 us
  waiting for transfers between devices  218 us (59%)
  matrix products  78.2 us (21%)
  local copies, waits for them, and re-layouts  31.2 us (8%)
  between operations  15.5 us (4%)
  other arithmetic  12.7 us (3%)
  starting transfers between devices  5.96 us (2%)
    reduce_scatter x1, waiting for transfers between devices, per_device(): lax.psum_scatter((outer_sum / total_rows).reshape(half_width * lax.axis_s...  126 us
    all_gather x1, waiting for transfers between devices, per_device(): shard_piece = lax.all_gather(conditioned[None], 'dp', axis=0, tiled=True)  49.6 us
    reduce_scatter x1, waiting for transfers between devices, per_device(): lax.psum_scatter(partial_value, 'mod', scatter_dimension=1, tiled=True)  36.3 us
    dot_general x1, matrix products, per_device(): jnp.einsum('rpa,rpb->pab', left_cols, right_cols, precision=highest, pref...  26.7 us
    dot_general x1, matrix products, per_device(): jnp.einsum('rnk,njk->rnj', chosen, shard_piece, precision=highest, prefer...  17.2 us
    dot_general x8, matrix products, per_device(): jnp.dot(inverse, system, precision=highest, preferred_element_type=jnp.fl...  16.8 us
    dot_general x8, matrix products, per_device(): jnp.dot(jnp.dot(inverse, system, precision=highest, preferred_element_typ...  15 us
    gather x1, local copies, waits for them, and re-layouts, per_device(): right_cols = jnp.take(train_grads, picked // 2, axis=1)  13.2 us
  transfers between devices with their start and end apart: 5, of which 4 were waited for; matrix products, arithmetic and copies ran while one was open for 0% of the time, Pallas kernels for 0%

commit v1 on v0

v1 whole, which is shorter than its diff:
```python
import functools
import math

import jax
import jax.numpy as jnp
from jax import lax
from jax.experimental import pallas as pl
from jax.experimental.pallas import tpu as pltpu
from jax.sharding import PartitionSpec as P

NEWTON_STEPS = 8
EPSILON = 1e-06

SIDE = 4
CHIPS = SIDE * SIDE
DEPTH = 8
WIDTH = 512
ROWS = 128
LANES = 128
TRI = 4 * LANES + 8
TOP = 264
HALF_Q = 64
BF16 = jnp.bfloat16
F32 = jnp.float32

RAW = 0
QRY = RAW + 16
R1 = QRY + 16
R2 = R1 + 4
R3 = R2 + 8
R4 = R3 + 2
EXC = R4 + 4
SEC = EXC + 1
FST = SEC + 4
PAR = FST + 16
ZED = PAR + 16
COPIES = ZED + 8


def split(value):
    high = value.astype(BF16)
    return high, (value - high.astype(F32)).astype(BF16)


def dot(a, b):
    return jnp.dot(a, b, preferred_element_type=F32)


def dot_t(a, b):
    return lax.dot_general(a, b, (((1,), (1,)), ((), ())), preferred_element_type=F32)


def wrap(i):
    return lax.rem(i + 2 * SIDE, SIDE)


def kernel(
    total_rows,
    scale,
    x_hbm,
    q_hbm,
    damp_ref,
    out_ref,
    x,
    q_in,
    stage,
    rx,
    qstage,
    qrx,
    part,
    r1,
    r2,
    r3,
    r4,
    half,
    p_ref,
    cond,
    g_hi,
    g_lo,
    acc,
    zout,
    zin,
    in_sem,
    send,
    recv,
):
    z = lax.axis_index("mod")
    dp = lax.axis_index("dp")
    core = lax.rem(dp, 2)
    chip = lax.div(dp, 2)
    cx = lax.div(chip, SIDE)
    cy = lax.rem(chip, SIDE)
    fst = cx * (1 - core) + cy * core
    snd = cy * (1 - core) + cx * core

    def chip_at(p, q, c=core):
        return (p * (1 - c) + q * c) * SIDE + q * (1 - c) + p * c

    def dev(p, q):
        return (z, chip_at(wrap(p), wrap(q)) * 2 + core)

    partner = (z, chip * 2 + 1 - core)

    def copy(src, dst, place, device):
        return pltpu.make_async_remote_copy(
            src_ref=src,
            dst_ref=dst,
            send_sem=send.at[place],
            recv_sem=recv.at[place],
            device_id=device,
            device_id_type=pl.DeviceIdType.MESH,
        )

    loads = []
    for lb in range(4):
        cols = pl.ds(lb * LANES, LANES)
        loads.append(pltpu.make_async_copy(x_hbm.at[:, cols], x.at[lb], in_sem.at[lb]))
        loads.append(pltpu.make_async_copy(q_hbm.at[:, cols], q_in.at[lb], in_sem.at[4 + lb]))
    for load in loads:
        load.start()

    barrier = pltpu.get_barrier_semaphore()

    def greet_chip(i, carry):
        there = lax.rem(chip + i, CHIPS)
        pl.semaphore_signal(
            barrier, inc=1, device_id=(z, there * 2 + core), device_id_type=pl.DeviceIdType.MESH
        )
        return carry

    lax.fori_loop(1, CHIPS, greet_chip, 0)

    def greet_layer(i, carry):
        pl.semaphore_signal(
            barrier, inc=1, device_id=(lax.rem(z + i, DEPTH), dp), device_id_type=pl.DeviceIdType.MESH
        )
        return carry

    lax.fori_loop(1, DEPTH, greet_layer, 0)
    pl.semaphore_signal(barrier, inc=1, device_id=partner, device_id_type=pl.DeviceIdType.MESH)
    for load in loads:
        load.wait()
    pl.semaphore_wait(barrier, CHIPS - 1 + DEPTH - 1 + 1)

    def second_of(b):
        return lax.rem(2 + 3 * b + lax.div(b, 2) * (3 - 2 * lax.rem(b, 2)), SIDE)

    def order(k):
        group = lax.div(k, 4)
        i = lax.rem(k, 4)
        odd = lax.rem(i, 2)
        is0 = lax.div(3 - group, 3)
        is1 = lax.rem(group, 2) * (1 - lax.div(group, 3))
        is3 = lax.div(group, 3)
        first = is0 * 2 + (1 - is0 - is3) * (1 + 2 * odd)
        b = i + is1 * (1 - 2 * odd)
        return first, b

    def module_of(k, c):
        first, b = order(k)
        p = cx * (1 - c) + cy * c
        q = cy * (1 - c) + cx * c
        return chip_at(lax.rem(p + first, SIDE), lax.rem(q + second_of(b), SIDE), c)

    def send_raw(k, carry):
        j = module_of(k, 1 - core)
        for lb in range(4):
            cols = pl.ds(lb * LANES, LANES)
            stage[j, :, cols] = x[lb, pl.ds(j, ROWS, stride=CHIPS), :]
        copy(stage.at[j], rx.at[j], RAW + k, partner).start()
        return carry

    lax.fori_loop(0, CHIPS, send_raw, 0)

    def stage_query(j, carry):
        for lb in range(4):
            cols = pl.ds(lb * LANES, LANES)
            rows = q_in[lb, pl.ds(j, 4, stride=CHIPS), :]
            qstage[j, :, cols] = jnp.concatenate([rows, rows], axis=0)
        return carry

    lax.fori_loop(0, CHIPS, stage_query, 0)

    def send_query(i, carry):
        there = lax.rem(chip + i, CHIPS)
        copy(qstage.at[there], qrx.at[chip], QRY + i, (z, there * 2 + core)).start()
        return carry

    lax.fori_loop(1, CHIPS, send_query, 0)
    qrx[chip] = qstage[chip]

    row_of = lax.broadcasted_iota(jnp.int32, (LANES, LANES), 0)
    col_of = lax.broadcasted_iota(jnp.int32, (LANES, LANES), 1)
    upper = row_of <= col_of
    eye = row_of == col_of

    def gram(k):
        j = module_of(k, core)
        copy(stage.at[j], rx.at[j], RAW + k, partner).wait_recv()
        blocks, highs, lows = [], [], []
        for lb in range(4):
            cols = pl.ds(pl.multiple_of(lax.rem(lb + core, 4) * LANES, LANES), LANES)
            block = jnp.concatenate([stage[j, :, cols], rx[j, :, cols]], axis=0)
            high, low = split(block)
            g_hi[j, :, cols] = high[:ROWS]
            g_lo[j, :, cols] = low[:ROWS]
            blocks.append(block)
            highs.append(high)
            lows.append(low)
        left = jnp.concatenate([blocks[0].T, blocks[2].T], axis=0)
        left_hi, left_lo = split(left)
        right_hi = jnp.concatenate(highs, axis=1)
        right_lo = jnp.concatenate(lows, axis=1)
        prod = dot(left_hi, right_hi) + (dot(left_hi, right_lo) + dot(left_lo, right_hi))
        first, second = prod[:LANES], prod[LANES:]
        one, two = first[:, :LANES], second[:, 2 * LANES : 3 * LANES]
        diagonal = jnp.sum(jnp.where(eye, two, 0.0), axis=0, keepdims=True)
        part[k, 0:128, :] = jnp.where(upper, one, two)
        part[k, 128:256, :] = first[:, LANES : 2 * LANES]
        part[k, 256:384, :] = second[:, 3 * LANES :]
        part[k, 384:512, :] = first[:, 2 * LANES : 3 * LANES]
        part[k, 512:520, :] = jnp.broadcast_to(diagonal, (8, LANES))

    def side(odd):
        return 1 - 2 * odd

    def far(i, carry):
        gram(i)
        copy(part.at[i], r1.at[i], R1 + i, dev(fst + side(lax.rem(i, 2)), snd)).start()
        return carry

    lax.fori_loop(0, 4, far, 0)

    def near(i, carry):
        k = 4 + i
        gram(k)
        odd = lax.rem(i, 2)
        slot = odd * 4 + i + 1 - 2 * odd
        copy(part.at[k], r2.at[slot], R2 + slot, dev(fst + side(odd), snd)).start()
        return carry

    lax.fori_loop(0, 4, near, 0)

    def rest(i, carry):
        gram(8 + i)
        return carry

    lax.fori_loop(0, 8, rest, 0)

    def joined(i, carry):
        k = 8 + i
        odd = lax.rem(i, 2)
        slot = odd * 4 + i
        copy(part.at[i], r1.at[i], R1 + i, partner).wait_recv()
        part[k] = part[k] + r1[i]
        copy(part.at[k], r2.at[slot], R2 + slot, dev(fst + side(odd), snd)).start()
        return carry

    lax.fori_loop(0, 4, joined, 0)

    def arrived(b):
        for s in (0, 4):
            copy(r2.at[s + b], r2.at[s + b], R2 + s + b, partner).wait_recv()
        part[12 + b] = part[12 + b] + r2[b] + r2[4 + b]

    top = pl.ds(0, TOP)
    low = pl.ds(TOP, TRI - TOP)
    plus = dev(fst, snd + 1)
    minus = dev(fst, snd - 1)

    def second_copy(b, rows, into, place, device):
        return copy(part.at[12 + b, rows], into.at[rows], place, device)

    arrived(0)
    far_top = second_copy(0, top, r3, R3, plus)
    far_low = second_copy(0, low, r3, R3 + 1, minus)
    far_top.start()
    far_low.start()
    arrived(1)
    near_low = second_copy(1, low, r4.at[0], R4 + 1, plus)
    near_low.start()
    arrived(2)
    near_top = second_copy(2, top, r4.at[1], R4 + 2, minus)
    near_top.start()
    far_top.wait_recv()
    part[13, top] = part[13, top] + r3[top]
    join_top = second_copy(1, top, r4.at[0], R4, plus)
    join_top.start()
    far_low.wait_recv()
    part[14, low] = part[14, low] + r3[low]
    join_low = second_copy(2, low, r4.at[1], R4 + 3, minus)
    join_low.start()
    arrived(3)
    near_low.wait_recv()
    near_top.wait_recv()
    join_top.wait_recv()
    join_low.wait_recv()
    half[core] = (part[15] + r4[0] + r4[1]) * (1.0 / total_rows)
    exchange = copy(half.at[core], half.at[core], EXC, partner)
    exchange.start()

    def wait_query(i, carry):
        copy(qstage.at[i], qrx.at[i], QRY + i, partner).wait_recv()
        return carry

    lax.fori_loop(1, CHIPS, wait_query, 0)
    sub = lax.broadcasted_iota(jnp.int32, (8, WIDTH), 0)
    query = jnp.concatenate(
        [jnp.where(sub < 4, qrx[2 * t], qrx[2 * t + 1]) for t in range(CHIPS // 2)], axis=0
    )
    copy(half.at[1 - core], half.at[1 - core], EXC, partner).wait_recv()

    def block_at(a, b):
        return pl.ds(a * LANES, LANES), pl.ds(b * LANES, LANES)

    squares = jnp.zeros((LANES, LANES), F32)
    traces = jnp.zeros((LANES, LANES), F32)
    diagonals = {}
    for h in range(2):
        b0, b1, b2, b3 = [(i + h) % 4 for i in range(4)]
        packed = half[h, 0:128, :]
        packed_t = packed.T
        spare = jnp.broadcast_to(half[h, 512:513, :], (LANES, LANES))
        diagonals[b0] = jnp.where(upper, packed, packed_t)
        diagonals[b2] = jnp.where(eye, spare, jnp.where(upper, packed_t, packed))
        for start, a, b in ((128, b0, b1), (256, b2, b3), (384, b0, b2)):
            block = half[h, start : start + LANES, :]
            squares = squares + 2.0 * (block * block)
            p_ref[block_at(a, b)] = block
            p_ref[block_at(b, a)] = block.T
    for block in diagonals.values():
        traces = traces + jnp.where(eye, block, 0.0)
    shift = damp_ref[chip] * jnp.sum(traces) / WIDTH
    for a, block in diagonals.items():
        block = block + jnp.where(eye, shift, 0.0)
        squares = squares + block * block
        p_ref[block_at(a, a)] = block
    scaled = jnp.full((8, LANES), jnp.sum(squares) + EPSILON, F32)
    unit = (1.0 / jnp.sqrt(scaled))[0:1, 0:1]
    p_ref[...] = p_ref[...] * unit
    cond[core, chip] = query * unit

    def newton(step, carry):
        value = p_ref[...]
        vector = cond[core, chip]
        high, low_ = split(value)
        v_high, v_low = split(vector)
        left_hi = jnp.concatenate([high, v_high], axis=0)
        left_lo = jnp.concatenate([low_, v_low], axis=0)
        prod = dot(left_hi, high) + (dot(left_hi, low_) + dot(left_lo, high))
        p_ref[...] = 2.0 * value - prod[:WIDTH]
        cond[core, chip] = 2.0 * vector - prod[WIDTH:]
        return carry

    lax.fori_loop(0, NEWTON_STEPS - 2, newton, 0)
    high, low_ = split(p_ref[...])

    def apply(vector):
        v_high, v_low = split(vector)
        return dot(v_high, high) + (dot(v_high, low_) + dot(v_low, high))

    vector = cond[core, chip]
    vector = 2.0 * vector - apply(vector)
    once = apply(vector)
    vector = 2.0 * vector - (2.0 * once - apply(once))
    cond[core, chip] = vector

    upper_q = pl.ds(0, HALF_Q // 2)
    lower_q = pl.ds(HALF_Q // 2, HALF_Q // 2)

    def whole(p, q):
        return cond.at[core, chip_at(wrap(p), wrap(q))]

    def rows_of(p, q, rows):
        return cond.at[core, chip_at(wrap(p), wrap(q)), rows]

    sent = []

    def go(ref, place, device):
        c = copy(ref, ref, place, device)
        c.start()
        sent.append(c)

    def come(ref, place):
        copy(ref, ref, place, partner).wait_recv()

    first_plus = dev(fst + 1, snd)
    first_minus = dev(fst - 1, snd)

    def score(c, j):
        v_high, v_low = split(cond[c, j])
        got = dot_t(v_high, g_hi[j]) + (dot_t(v_high, g_lo[j]) + dot_t(v_low, g_hi[j]))
        rows = pl.ds(pl.multiple_of(c * HALF_Q, HALF_Q), HALF_Q)
        acc[rows, :] = acc[rows, :] + got

    def place_par(a, b):
        return PAR + a * 4 + b

    def hand_over(a, b):
        go(whole(fst + a, snd + b), place_par(a, b), partner)

    acc[...] = jnp.zeros((2 * HALF_Q, ROWS), F32)

    def along_first(b):
        go(whole(fst, snd + b), FST + 4 * b, first_plus)
        go(whole(fst, snd + b), FST + 4 * b + 1, first_minus)

    go(whole(fst, snd), SEC, plus)
    go(whole(fst, snd), SEC + 1, minus)
    along_first(0)
    hand_over(0, 0)
    come(whole(fst, snd - 1), SEC)
    go(rows_of(fst, snd - 1, upper_q), SEC + 2, plus)
    along_first(3)
    hand_over(0, 3)
    come(whole(fst, snd + 1), SEC + 1)
    go(rows_of(fst, snd + 1, lower_q), SEC + 3, minus)
    along_first(1)
    hand_over(0, 1)

    def first_near(b):
        come(whole(fst - 1, snd + b), FST + 4 * b)
        go(rows_of(fst - 1, snd + b, upper_q), FST + 4 * b + 2, first_plus)
        hand_over(3, b)
        come(whole(fst + 1, snd + b), FST + 4 * b + 1)
        go(rows_of(fst + 1, snd + b, lower_q), FST + 4 * b + 3, first_minus)
        hand_over(1, b)

    def first_far(b):
        come(rows_of(fst + 2, snd + b, upper_q), FST + 4 * b + 2)
        come(rows_of(fst + 2, snd + b, lower_q), FST + 4 * b + 3)
        hand_over(2, b)

    def own_scores(a, b):
        score(core, chip_at(wrap(fst + a), wrap(snd + b)))

    first_near(0)
    come(rows_of(fst, snd + 2, upper_q), SEC + 2)
    come(rows_of(fst, snd + 2, lower_q), SEC + 3)
    along_first(2)
    hand_over(0, 2)
    for b in (0, 3, 1, 2):
        own_scores(0, b)
    own_scores(1, 0)
    own_scores(3, 0)
    for before, b in ((0, 3), (3, 1), (1, 2)):
        first_near(b)
        first_far(before)
        own_scores(1, b)
        own_scores(3, b)
        own_scores(2, before)
    first_far(2)
    own_scores(2, 2)

    def other(a, b):
        c = 1 - core
        j = chip_at(wrap(snd + a), wrap(fst + b), c)
        come(cond.at[c, j], place_par(a, b))
        score(c, j)

    for b in (0, 3, 1):
        other(0, b)
    other(3, 0)
    other(1, 0)
    other(0, 2)
    for before, b in ((0, 3), (3, 1), (1, 2)):
        other(3, b)
        other(1, b)
        other(2, before)
    other(2, 2)

    done = acc[...] * scale
    for h in range(2):
        zout[:, 8 * h : 8 * h + 8, :] = done[h * HALF_Q : (h + 1) * HALF_Q].reshape(DEPTH, 8, ROWS)

    def send_scores(i, carry):
        there = lax.rem(z + i, DEPTH)
        copy(zout.at[there], zin.at[i], ZED + i, (there, dp)).start()
        return carry

    lax.fori_loop(1, DEPTH, send_scores, 0)
    total = zout[z]
    for i in range(1, DEPTH):
        copy(zin.at[i], zin.at[i], ZED + i, partner).wait_recv()
        total = total + zin[i]
    out_ref[...] = jnp.concatenate([total[0:4], total[8:12], total[4:8], total[12:16]], axis=0)

    def sent_raw(k, carry):
        copy(stage.at[0], rx.at[0], RAW + k, partner).wait_send()
        return carry

    lax.fori_loop(0, CHIPS, sent_raw, 0)

    def sent_query(i, carry):
        copy(qstage.at[0], qrx.at[0], QRY + i, partner).wait_send()
        return carry

    lax.fori_loop(1, CHIPS, sent_query, 0)

    def sent_part(i, carry):
        copy(part.at[0], r2.at[0], R1 + i, partner).wait_send()
        return carry

    lax.fori_loop(0, 12, sent_part, 0)
    for c in (far_top, far_low, near_low, near_top, join_top, join_low, exchange, *sent):
        c.wait_send()

    def sent_scores(i, carry):
        copy(zout.at[0], zin.at[0], ZED + i, partner).wait_send()
        return carry

    lax.fori_loop(1, DEPTH, sent_scores, 0)


def per_device(train_grads, queries, damping):
    rows, modules, width = train_grads.shape
    total_rows = rows * lax.axis_size("dp")
    scale = 1.0 / math.sqrt(modules * lax.axis_size("mod") * width)
    vmem = pltpu.VMEM
    out = pl.pallas_call(
        functools.partial(kernel, total_rows, scale),
        out_shape=jax.ShapeDtypeStruct((16, ROWS), F32),
        in_specs=[
            pl.BlockSpec(memory_space=pl.ANY),
            pl.BlockSpec(memory_space=pl.ANY),
            pl.BlockSpec(memory_space=pltpu.SMEM),
        ],
        out_specs=pl.BlockSpec(memory_space=vmem),
        scratch_shapes=[
            vmem((4, ROWS * CHIPS, LANES), F32),
            vmem((4, 4 * CHIPS, LANES), F32),
            vmem((CHIPS, ROWS, WIDTH), F32),
            vmem((CHIPS, ROWS, WIDTH), F32),
            vmem((CHIPS, 8, WIDTH), F32),
            vmem((CHIPS, 8, WIDTH), F32),
            vmem((CHIPS, TRI, LANES), F32),
            vmem((4, TRI, LANES), F32),
            vmem((8, TRI, LANES), F32),
            vmem((TRI, LANES), F32),
            vmem((2, TRI, LANES), F32),
            vmem((2, TRI, LANES), F32),
            vmem((WIDTH, WIDTH), F32),
            vmem((2, CHIPS, HALF_Q, WIDTH), F32),
            vmem((CHIPS, ROWS, WIDTH), BF16),
            vmem((CHIPS, ROWS, WIDTH), BF16),
            vmem((2 * HALF_Q, ROWS), F32),
            vmem((DEPTH, 16, ROWS), F32),
            vmem((DEPTH, 16, ROWS), F32),
            pltpu.SemaphoreType.DMA((8,)),
            pltpu.SemaphoreType.DMA((COPIES,)),
            pltpu.SemaphoreType.DMA((COPIES,)),
        ],
        compiler_params=pltpu.CompilerParams(
            collective_id=0, has_side_effects=True, vmem_limit_bytes=60 * 2**20
        ),
    )(train_grads.reshape(rows * modules, width), queries.reshape(-1, width), damping)
    return out.T


def solution(mesh):
    return jax.shard_map(
        per_device,
        mesh=mesh,
        in_specs=(P("dp", "mod", None), P("dp", "mod", None), P("mod")),
        out_specs=P("dp", "mod"),
        check_vma=False,
    )
```

time: 368 us -> 81.7 us (0.22); the launches traced: 361 us -> 81.5 us
  waiting for transfers between devices: 218 us -> 0 us
  Pallas kernels: 0 us -> 80.2 us
  matrix products: 78.2 us -> 0 us
  local copies, waits for them, and re-layouts: 31.2 us -> 1.3 us
  between operations: 15.5 us -> 0.01 us
  other arithmetic: 12.7 us -> 0 us
  starting transfers between devices: 5.96 us -> 0 us
    reduce_scatter x2 -> x0, waiting for transfers between devices: 162 us -> none  [the longest x1 126 us: per_device(): lax.psum_scatter((outer_sum / total_rows).reshape(half_width * lax.axis_s...]
    pallas_call x0 -> x1, Pallas kernels: none -> 80.2 us  [per_device(): pl.pallas_call(functools.partial(kernel, total_rows, scale), out_shape=ja...]
    dot_general x20 -> x0, matrix products: 78.2 us -> none  [the longest x1 26.7 us: per_device(): jnp.einsum('rpa,rpb->pab', left_cols, right_cols, precision=highest, pref...]
    all_gather x1 -> x0, waiting for transfers between devices: 49.6 us -> none  [per_device(): shard_piece = lax.all_gather(conditioned[None], 'dp', axis=0, tiled=True)]
    gather x2 -> x0, local copies, waits for them, and re-layouts: 18.1 us -> none  [the longest x1 13.2 us: per_device(): right_cols = jnp.take(train_grads, picked // 2, axis=1)]
    select_n x3 -> x0, other arithmetic: 8.63 us -> none  [the longest x2 8.63 us: per_device(): right_cols = jnp.take(train_grads, picked // 2, axis=1)]
    reshape x2 -> x0, local copies, waits for them, and re-layouts: 6.35 us -> none  [the longest x1 5.6 us: per_device(): paired = train_grads.reshape(rows_dev, group_mods * 2, half_width)]
    all_to_all x1 -> x0, waiting for transfers between devices: 5.79 us -> none  [per_device(): lax.all_to_all(outgoing, 'dp', split_axis=0, concat_axis=1, tiled=True)[0]]
  transfers between devices with their start and end apart: 5 -> 0, of which waited for: 4 -> 0; matrix products, arithmetic and copies ran while one was open for 0% -> 0% of each run, Pallas kernels for 0% -> 0%
where the time goes in v1:
time: 81.7 us; the launch traced here: 81.5 us
  Pallas kernels  80.2 us (98%)
  local copies, waits for them, and re-layouts  1.3 us (2%)
    pallas_call x1, Pallas kernels, per_device(): pl.pallas_call(functools.partial(kernel, total_rows, scale), out_shape=ja...  80.2 us

profile of v1, /device:TPU:2, one launch (start us, length us, event | category | flops | bytes accessed | tf_op | source)
XLA Modules:
  0.0 81.5 jit_solution(2572182704830989867)
XLA Ops:
  0.0 80.2 %shard_map.37 = f32[16,128]{1,0:T(8,128)} custom-call(f32[2048,512]{1,0:T(8,128)} %bitcast.3, f32[64,512]{1,0:T(8,128)} %bitcast.4, f32[16]{0:T(128)} %damp_ref.1), custom_call_target="tpu_custom_call" | custom-call | tf_op jit(solution)/shard_map/pallas_call | solution.py:520
  80.2 1.3 %copy.5 = f32[128,16]{0,1:T(8,128)} copy(f32[128,16]{0,1:T(8,128)} %bitcast.5) | data formatting | bytes 16384

commit v2 on v1

--- a/solution.py
+++ b/solution.py
@@ -17,6 +17,7 @@
 WIDTH = 512
 ROWS = 128
 LANES = 128
+MID = WIDTH // 2
 TRI = 4 * LANES + 8
 TOP = 264
 HALF_Q = 64
@@ -31,8 +32,8 @@
 R4 = R3 + 2
 EXC = R4 + 4
 SEC = EXC + 1
-FST = SEC + 4
-PAR = FST + 16
+FST = SEC + 6
+PAR = FST + 24
 ZED = PAR + 16
 COPIES = ZED + 8
 
@@ -75,8 +76,7 @@
     half,
     p_ref,
     cond,
-    g_hi,
-    g_lo,
+    grads,
     acc,
     zout,
     zin,
@@ -138,22 +138,17 @@
 
     lax.fori_loop(1, DEPTH, greet_layer, 0)
     pl.semaphore_signal(barrier, inc=1, device_id=partner, device_id_type=pl.DeviceIdType.MESH)
-    for load in loads:
-        load.wait()
-    pl.semaphore_wait(barrier, CHIPS - 1 + DEPTH - 1 + 1)
-
     def second_of(b):
         return lax.rem(2 + 3 * b + lax.div(b, 2) * (3 - 2 * lax.rem(b, 2)), SIDE)
 
     def order(k):
-        group = lax.div(k, 4)
-        i = lax.rem(k, 4)
-        odd = lax.rem(i, 2)
-        is0 = lax.div(3 - group, 3)
-        is1 = lax.rem(group, 2) * (1 - lax.div(group, 3))
-        is3 = lax.div(group, 3)
-        first = is0 * 2 + (1 - is0 - is3) * (1 + 2 * odd)
-        b = i + is1 * (1 - 2 * odd)
+        is0 = lax.div(CHIPS - 1 - k, 12)
+        is3 = lax.div(k, 12)
+        i = (k - 4) * (1 - is0) * (1 - is3)
+        first = is0 * 2 + (1 - is0 - is3) * (1 + 2 * lax.rem(i, 2))
+        late = lax.div(i, 4)
+        middle = late * lax.div(i, 2) + (1 - late) * (1 - lax.rem(lax.div(i + 1, 2), 2))
+        b = (is0 + is3) * lax.rem(k, 4) + (1 - is0 - is3) * middle
         return first, b
 
     def module_of(k, c):
@@ -162,24 +157,24 @@
         q = cy * (1 - c) + cx * c
         return chip_at(lax.rem(p + first, SIDE), lax.rem(q + second_of(b), SIDE), c)
 
+    for load in loads:
+        load.wait()
+
+    def stage_module(j, carry):
+        for lb in range(4):
+            stage[j, :, pl.ds(lb * LANES, LANES)] = x[lb, pl.ds(j, ROWS, stride=CHIPS), :]
+            qstage[j, pl.ds(lb * 4, 4), :] = q_in[lb, pl.ds(j, 4, stride=CHIPS), :]
+        return carry
+
+    lax.fori_loop(0, CHIPS, stage_module, 0)
+    pl.semaphore_wait(barrier, CHIPS - 1 + DEPTH - 1 + 1)
+
     def send_raw(k, carry):
         j = module_of(k, 1 - core)
-        for lb in range(4):
-            cols = pl.ds(lb * LANES, LANES)
-            stage[j, :, cols] = x[lb, pl.ds(j, ROWS, stride=CHIPS), :]
         copy(stage.at[j], rx.at[j], RAW + k, partner).start()
         return carry
 
-    lax.fori_loop(0, CHIPS, send_raw, 0)
-
-    def stage_query(j, carry):
-        for lb in range(4):
-            cols = pl.ds(lb * LANES, LANES)
-            rows = q_in[lb, pl.ds(j, 4, stride=CHIPS), :]
-            qstage[j, :, cols] = jnp.concatenate([rows, rows], axis=0)
-        return carry
-
-    lax.fori_loop(0, CHIPS, stage_query, 0)
+    lax.fori_loop(0, 4, send_raw, 0)
 
     def send_query(i, carry):
         there = lax.rem(chip + i, CHIPS)
@@ -187,6 +182,7 @@
         return carry
 
     lax.fori_loop(1, CHIPS, send_query, 0)
+    lax.fori_loop(4, CHIPS, send_raw, 0)
     qrx[chip] = qstage[chip]
 
     row_of = lax.broadcasted_iota(jnp.int32, (LANES, LANES), 0)
@@ -202,8 +198,8 @@
             cols = pl.ds(pl.multiple_of(lax.rem(lb + core, 4) * LANES, LANES), LANES)
             block = jnp.concatenate([stage[j, :, cols], rx[j, :, cols]], axis=0)
             high, low = split(block)
-            g_hi[j, :, cols] = high[:ROWS]
-            g_lo[j, :, cols] = low[:ROWS]
+            grads[j, :ROWS, cols] = high[:ROWS]
+            grads[j, ROWS:, cols] = low[:ROWS]
             blocks.append(block)
             highs.append(high)
             lows.append(low)
@@ -231,37 +227,48 @@
 
     lax.fori_loop(0, 4, far, 0)
 
-    def near(i, carry):
-        k = 4 + i
-        gram(k)
-        odd = lax.rem(i, 2)
-        slot = odd * 4 + i + 1 - 2 * odd
-        copy(part.at[k], r2.at[slot], R2 + slot, dev(fst + side(odd), snd)).start()
-        return carry
-
-    lax.fori_loop(0, 4, near, 0)
-
-    def rest(i, carry):
-        gram(8 + i)
-        return carry
-
-    lax.fori_loop(0, 8, rest, 0)
-
-    def joined(i, carry):
-        k = 8 + i
-        odd = lax.rem(i, 2)
-        slot = odd * 4 + i
+    def grams(low, high):
+        def step(k, carry):
+            gram(k)
+            return carry
+
+        lax.fori_loop(low, high, step, 0)
+
+    def near(k, slot):
+        copy(part.at[k], r2.at[slot], R2 + slot, dev(fst + (1 if slot < 4 else -1), snd)).start()
+
+    def joined(k, i, slot):
         copy(part.at[i], r1.at[i], R1 + i, partner).wait_recv()
         part[k] = part[k] + r1[i]
-        copy(part.at[k], r2.at[slot], R2 + slot, dev(fst + side(odd), snd)).start()
-        return carry
-
-    lax.fori_loop(0, 4, joined, 0)
+        near(k, slot)
+
+    grams(4, 5)
+    near(4, 1)
+    grams(5, 6)
+    near(5, 4)
+    grams(6, 12)
+    joined(6, 0, 0)
+    joined(7, 1, 5)
+    near(9, 6)
+    grams(12, 16)
+    joined(8, 2, 2)
+    near(10, 3)
+    joined(11, 3, 7)
 
     def arrived(b):
         for s in (0, 4):
             copy(r2.at[s + b], r2.at[s + b], R2 + s + b, partner).wait_recv()
         part[12 + b] = part[12 + b] + r2[b] + r2[4 + b]
+
+    def wait_query(i, carry):
+        copy(qstage.at[i], qrx.at[i], QRY + i, partner).wait_recv()
+        return carry
+
+    lax.fori_loop(1, CHIPS, wait_query, 0)
+    for lb in range(4):
+        cond[core, chip, :, lb * LANES : (lb + 1) * LANES] = jnp.concatenate(
+            [qrx[i, lb * 4 : lb * 4 + 4, :] for i in range(CHIPS)], axis=0
+        )
 
     top = pl.ds(0, TOP)
     low = pl.ds(TOP, TRI - TOP)
@@ -299,15 +306,6 @@
     exchange = copy(half.at[core], half.at[core], EXC, partner)
     exchange.start()
 
-    def wait_query(i, carry):
-        copy(qstage.at[i], qrx.at[i], QRY + i, partner).wait_recv()
-        return carry
-
-    lax.fori_loop(1, CHIPS, wait_query, 0)
-    sub = lax.broadcasted_iota(jnp.int32, (8, WIDTH), 0)
-    query = jnp.concatenate(
-        [jnp.where(sub < 4, qrx[2 * t], qrx[2 * t + 1]) for t in range(CHIPS // 2)], axis=0
-    )
     copy(half.at[1 - core], half.at[1 - core], EXC, partner).wait_recv()
 
     def block_at(a, b):
@@ -338,18 +336,23 @@
     scaled = jnp.full((8, LANES), jnp.sum(squares) + EPSILON, F32)
     unit = (1.0 / jnp.sqrt(scaled))[0:1, 0:1]
     p_ref[...] = p_ref[...] * unit
-    cond[core, chip] = query * unit
+    cond[core, chip] = cond[core, chip] * unit
 
     def newton(step, carry):
         value = p_ref[...]
         vector = cond[core, chip]
         high, low_ = split(value)
         v_high, v_low = split(vector)
-        left_hi = jnp.concatenate([high, v_high], axis=0)
-        left_lo = jnp.concatenate([low_, v_low], axis=0)
+        left_hi = jnp.concatenate([high[:MID], v_high], axis=0)
+        left_lo = jnp.concatenate([low_[:MID], v_low], axis=0)
         prod = dot(left_hi, high) + (dot(left_hi, low_) + dot(left_lo, high))
-        p_ref[...] = 2.0 * value - prod[:WIDTH]
-        cond[core, chip] = 2.0 * vector - prod[WIDTH:]
+        hi_r, lo_r = high[:, MID:], low_[:, MID:]
+        corner = dot(high[MID:], hi_r) + (dot(high[MID:], lo_r) + dot(low_[MID:], hi_r))
+        upper_rows = 2.0 * value[:MID] - prod[:MID]
+        p_ref[:MID, :] = upper_rows
+        p_ref[MID:, :MID] = upper_rows[:, MID:].T
+        p_ref[MID:, MID:] = 2.0 * value[MID:, MID:] - corner
+        cond[core, chip] = 2.0 * vector - prod[MID:]
         return carry
 
     lax.fori_loop(0, NEWTON_STEPS - 2, newton, 0)
@@ -365,16 +368,14 @@
     vector = 2.0 * vector - (2.0 * once - apply(once))
     cond[core, chip] = vector
 
-    upper_q = pl.ds(0, HALF_Q // 2)
-    lower_q = pl.ds(HALF_Q // 2, HALF_Q // 2)
-
-    def whole(p, q):
-        return cond.at[core, chip_at(wrap(p), wrap(q))]
-
-    def rows_of(p, q, rows):
-        return cond.at[core, chip_at(wrap(p), wrap(q)), rows]
-
+    halves = (pl.ds(0, HALF_Q // 2), pl.ds(HALF_Q // 2, HALF_Q // 2))
+    first_to = (dev(fst + 1, snd), dev(fst - 1, snd))
+    second_to = (plus, minus)
     sent = []
+
+    def at(a, b, rows=None):
+        ref = cond.at[core, chip_at(wrap(fst + a), wrap(snd + b))]
+        return ref if rows is None else ref.at[rows]
 
     def go(ref, place, device):
         c = copy(ref, ref, place, device)
@@ -384,90 +385,102 @@
     def come(ref, place):
         copy(ref, ref, place, partner).wait_recv()
 
-    first_plus = dev(fst + 1, snd)
-    first_minus = dev(fst - 1, snd)
+    def hand_over(a, b):
+        go(at(a, b), PAR + a * 4 + b, partner)
+
+    def both_ways(a, b, place, devices):
+        for n in range(2):
+            for way in range(2):
+                h = n ^ way
+                go(at(a, b, halves[h]), place + 2 * way + n, devices[way])
+
+    def along_first(b):
+        both_ways(0, b, FST + 6 * b, first_to)
+
+    def pass_first(b):
+        for way in range(2):
+            come(at(3 - 2 * way, b, halves[way]), FST + 6 * b + 2 * way)
+            go(at(3 - 2 * way, b, halves[way]), FST + 6 * b + 4 + way, first_to[way])
+
+    def rest_first(b):
+        for way in range(2):
+            come(at(3 - 2 * way, b, halves[1 - way]), FST + 6 * b + 2 * way + 1)
+            hand_over(3 - 2 * way, b)
+
+    def far_first(b):
+        for way in range(2):
+            come(at(2, b, halves[way]), FST + 6 * b + 4 + way)
+        hand_over(2, b)
 
     def score(c, j):
-        v_high, v_low = split(cond[c, j])
-        got = dot_t(v_high, g_hi[j]) + (dot_t(v_high, g_lo[j]) + dot_t(v_low, g_hi[j]))
+        left = jnp.concatenate(split(cond[c, j]), axis=0)
+        got = dot_t(left, grads[j])
+        got = got[:, :ROWS] + got[:, ROWS:]
         rows = pl.ds(pl.multiple_of(c * HALF_Q, HALF_Q), HALF_Q)
-        acc[rows, :] = acc[rows, :] + got
-
-    def place_par(a, b):
-        return PAR + a * 4 + b
-
-    def hand_over(a, b):
-        go(whole(fst + a, snd + b), place_par(a, b), partner)
-
-    acc[...] = jnp.zeros((2 * HALF_Q, ROWS), F32)
-
-    def along_first(b):
-        go(whole(fst, snd + b), FST + 4 * b, first_plus)
-        go(whole(fst, snd + b), FST + 4 * b + 1, first_minus)
-
-    go(whole(fst, snd), SEC, plus)
-    go(whole(fst, snd), SEC + 1, minus)
-    along_first(0)
-    hand_over(0, 0)
-    come(whole(fst, snd - 1), SEC)
-    go(rows_of(fst, snd - 1, upper_q), SEC + 2, plus)
-    along_first(3)
-    hand_over(0, 3)
-    come(whole(fst, snd + 1), SEC + 1)
-    go(rows_of(fst, snd + 1, lower_q), SEC + 3, minus)
-    along_first(1)
-    hand_over(0, 1)
-
-    def first_near(b):
-        come(whole(fst - 1, snd + b), FST + 4 * b)
-        go(rows_of(fst - 1, snd + b, upper_q), FST + 4 * b + 2, first_plus)
-        hand_over(3, b)
-        come(whole(fst + 1, snd + b), FST + 4 * b + 1)
-        go(rows_of(fst + 1, snd + b, lower_q), FST + 4 * b + 3, first_minus)
-        hand_over(1, b)
-
-    def first_far(b):
-        come(rows_of(fst + 2, snd + b, upper_q), FST + 4 * b + 2)
-        come(rows_of(fst + 2, snd + b, lower_q), FST + 4 * b + 3)
-        hand_over(2, b)
-
-    def own_scores(a, b):
+        acc[rows, :] = acc[rows, :] + (got[:HALF_Q] + got[HALF_Q:])
+
+    def own(a, b):
         score(core, chip_at(wrap(fst + a), wrap(snd + b)))
-
-    first_near(0)
-    come(rows_of(fst, snd + 2, upper_q), SEC + 2)
-    come(rows_of(fst, snd + 2, lower_q), SEC + 3)
-    along_first(2)
-    hand_over(0, 2)
-    for b in (0, 3, 1, 2):
-        own_scores(0, b)
-    own_scores(1, 0)
-    own_scores(3, 0)
-    for before, b in ((0, 3), (3, 1), (1, 2)):
-        first_near(b)
-        first_far(before)
-        own_scores(1, b)
-        own_scores(3, b)
-        own_scores(2, before)
-    first_far(2)
-    own_scores(2, 2)
 
     def other(a, b):
         c = 1 - core
         j = chip_at(wrap(snd + a), wrap(fst + b), c)
-        come(cond.at[c, j], place_par(a, b))
+        come(cond.at[c, j], PAR + a * 4 + b)
         score(c, j)
 
-    for b in (0, 3, 1):
-        other(0, b)
+    acc[...] = jnp.zeros((2 * HALF_Q, ROWS), F32)
+    both_ways(0, 0, SEC, second_to)
+    along_first(0)
+    hand_over(0, 0)
+    for way in range(2):
+        come(at(0, 3 - 2 * way, halves[way]), SEC + 2 * way)
+        go(at(0, 3 - 2 * way, halves[way]), SEC + 4 + way, second_to[way])
+    for way in range(2):
+        come(at(0, 3 - 2 * way, halves[1 - way]), SEC + 2 * way + 1)
+        along_first(3 - 2 * way)
+        hand_over(0, 3 - 2 * way)
+    pass_first(0)
+    rest_first(0)
+    own(0, 0)
+    for way in range(2):
+        come(at(0, 2, halves[way]), SEC + 4 + way)
+    along_first(2)
+    hand_over(0, 2)
+    own(0, 3)
+    own(0, 1)
+    other(0, 0)
+    pass_first(3)
+    rest_first(3)
+    own(0, 2)
+    own(3, 0)
+    pass_first(1)
+    rest_first(1)
+    own(1, 0)
+    other(0, 3)
+    far_first(0)
+    other(0, 1)
+    pass_first(2)
+    rest_first(2)
+    own(3, 3)
+    own(1, 3)
     other(3, 0)
     other(1, 0)
+    far_first(3)
+    own(3, 1)
+    own(1, 1)
     other(0, 2)
-    for before, b in ((0, 3), (3, 1), (1, 2)):
-        other(3, b)
-        other(1, b)
-        other(2, before)
-    other(2, 2)
+    far_first(1)
+    own(2, 0)
+    other(3, 3)
+    other(1, 3)
+    far_first(2)
+    for a, b in ((3, 2), (1, 2), (2, 3), (2, 1)):
+        own(a, b)
+    for a, b in ((3, 1), (1, 1), (2, 0), (3, 2), (1, 2)):
+        other(a, b)
+    own(2, 2)
+    for b in (3, 1, 2):
+        other(2, b)
 
     done = acc[...] * scale
     for h in range(2):
@@ -531,8 +544,8 @@
             vmem((4, 4 * CHIPS, LANES), F32),
             vmem((CHIPS, ROWS, WIDTH), F32),
             vmem((CHIPS, ROWS, WIDTH), F32),
-            vmem((CHIPS, 8, WIDTH), F32),
-            vmem((CHIPS, 8, WIDTH), F32),
+            vmem((CHIPS, 16, LANES), F32),
+            vmem((CHIPS, 16, LANES), F32),
             vmem((CHIPS, TRI, LANES), F32),
             vmem((4, TRI, LANES), F32),
             vmem((8, TRI, LANES), F32),
@@ -541,8 +554,7 @@
             vmem((2, TRI, LANES), F32),
             vmem((WIDTH, WIDTH), F32),
             vmem((2, CHIPS, HALF_Q, WIDTH), F32),
-            vmem((CHIPS, ROWS, WIDTH), BF16),
-            vmem((CHIPS, ROWS, WIDTH), BF16),
+            vmem((CHIPS, 2 * ROWS, WIDTH), BF16),
             vmem((2 * HALF_Q, ROWS), F32),
             vmem((DEPTH, 16, ROWS), F32),
             vmem((DEPTH, 16, ROWS), F32),

time: 81.7 us -> 73.9 us (0.905)
  Pallas kernels: 80.2 us -> 72.3 us
    pallas_call x1, Pallas kernels: 80.2 us -> 72.3 us  [per_device(): pl.pallas_call(functools.partial(kernel, total_rows, scale), out_shape=ja...]
where the time goes in v2:
time: 73.9 us; the launch traced here: 73.6 us
  Pallas kernels  72.3 us (98%)
  local copies, waits for them, and re-layouts  1.3 us (2%)
    pallas_call x1, Pallas kernels, per_device(): pl.pallas_call(functools.partial(kernel, total_rows, scale), out_shape=ja...  72.3 us

profile of v2, /device:TPU:2, one launch (start us, length us, event | category | flops | bytes accessed | tf_op | source)
XLA Modules:
  0.0 73.6 jit_solution(8200465149833148868)
XLA Ops:
  0.0 72.3 %shard_map.37 = f32[16,128]{1,0:T(8,128)} custom-call(f32[2048,512]{1,0:T(8,128)} %bitcast.3, f32[64,512]{1,0:T(8,128)} %bitcast.4, f32[16]{0:T(128)} %damp_ref.1), custom_call_target="tpu_custom_call" | custom-call | tf_op jit(solution)/shard_map/pallas_call | solution.py:533
  72.3 1.3 %copy.5 = f32[128,16]{0,1:T(8,128)} copy(f32[128,16]{0,1:T(8,128)} %bitcast.5) | data formatting | bytes 16384

commit v3 on v2

--- a/solution.py
+++ b/solution.py
@@ -160,13 +160,22 @@
     for load in loads:
         load.wait()
 
-    def stage_module(j, carry):
+    def stage_rows(k):
+        j = module_of(k, 1 - core)
         for lb in range(4):
             stage[j, :, pl.ds(lb * LANES, LANES)] = x[lb, pl.ds(j, ROWS, stride=CHIPS), :]
+
+    def stage_first(k, carry):
+        stage_rows(k)
+        return carry
+
+    def stage_query(j, carry):
+        for lb in range(4):
             qstage[j, pl.ds(lb * 4, 4), :] = q_in[lb, pl.ds(j, 4, stride=CHIPS), :]
         return carry
 
-    lax.fori_loop(0, CHIPS, stage_module, 0)
+    lax.fori_loop(0, 4, stage_first, 0)
+    lax.fori_loop(0, CHIPS, stage_query, 0)
     pl.semaphore_wait(barrier, CHIPS - 1 + DEPTH - 1 + 1)
 
     def send_raw(k, carry):
@@ -174,6 +183,10 @@
         copy(stage.at[j], rx.at[j], RAW + k, partner).start()
         return carry
 
+    def stage_and_send(k, carry):
+        stage_rows(k)
+        return send_raw(k, carry)
+
     lax.fori_loop(0, 4, send_raw, 0)
 
     def send_query(i, carry):
@@ -182,7 +195,7 @@
         return carry
 
     lax.fori_loop(1, CHIPS, send_query, 0)
-    lax.fori_loop(4, CHIPS, send_raw, 0)
+    lax.fori_loop(4, CHIPS, stage_and_send, 0)
     qrx[chip] = qstage[chip]
 
     row_of = lax.broadcasted_iota(jnp.int32, (LANES, LANES), 0)
@@ -338,6 +351,11 @@
     p_ref[...] = p_ref[...] * unit
     cond[core, chip] = cond[core, chip] * unit
 
+    def twice(a_high, a_low, b_high, b_low):
+        both = dot(jnp.concatenate([a_high, a_low], axis=0), b_high)
+        rows = a_high.shape[0]
+        return both[:rows] + (both[rows:] + dot(a_high, b_low))
+
     def newton(step, carry):
         value = p_ref[...]
         vector = cond[core, chip]
@@ -345,9 +363,8 @@
         v_high, v_low = split(vector)
         left_hi = jnp.concatenate([high[:MID], v_high], axis=0)
         left_lo = jnp.concatenate([low_[:MID], v_low], axis=0)
-        prod = dot(left_hi, high) + (dot(left_hi, low_) + dot(left_lo, high))
-        hi_r, lo_r = high[:, MID:], low_[:, MID:]
-        corner = dot(high[MID:], hi_r) + (dot(high[MID:], lo_r) + dot(low_[MID:], hi_r))
+        prod = twice(left_hi, left_lo, high, low_)
+        corner = twice(high[MID:], low_[MID:], high[:, MID:], low_[:, MID:])
         upper_rows = 2.0 * value[:MID] - prod[:MID]
         p_ref[:MID, :] = upper_rows
         p_ref[MID:, :MID] = upper_rows[:, MID:].T
@@ -355,12 +372,13 @@
         cond[core, chip] = 2.0 * vector - prod[MID:]
         return carry
 
-    lax.fori_loop(0, NEWTON_STEPS - 2, newton, 0)
+    for step in range(NEWTON_STEPS - 2):
+        newton(step, 0)
     high, low_ = split(p_ref[...])
 
     def apply(vector):
         v_high, v_low = split(vector)
-        return dot(v_high, high) + (dot(v_high, low_) + dot(v_low, high))
+        return twice(v_high, v_low, high, low_)
 
     vector = cond[core, chip]
     vector = 2.0 * vector - apply(vector)
@@ -471,16 +489,17 @@
     other(0, 2)
     far_first(1)
     own(2, 0)
-    other(3, 3)
-    other(1, 3)
+    for a, b in ((3, 2), (1, 2), (2, 3)):
+        own(a, b)
+    for a, b in ((3, 3), (1, 3), (3, 1)):
+        other(a, b)
     far_first(2)
-    for a, b in ((3, 2), (1, 2), (2, 3), (2, 1)):
-        own(a, b)
-    for a, b in ((3, 1), (1, 1), (2, 0), (3, 2), (1, 2)):
+    own(2, 1)
+    other(1, 1)
+    other(2, 0)
+    own(2, 2)
+    for a, b in ((3, 2), (1, 2), (2, 3), (2, 1), (2, 2)):
         other(a, b)
-    own(2, 2)
-    for b in (3, 1, 2):
-        other(2, b)
 
     done = acc[...] * scale
     for h in range(2):

time: 73.9 us -> 73.2 us (level); the launches traced: 73.6 us -> 72.1 us
  Pallas kernels: 72.3 us -> 70.8 us
    pallas_call x1, Pallas kernels: 72.3 us -> 70.8 us  [per_device(): pl.pallas_call(functools.partial(kernel, total_rows, scale), out_shape=ja...]
where the time goes in v3:
time: 73.2 us; the launch traced here: 72.1 us
  Pallas kernels  70.8 us (97%)
  local copies, waits for them, and re-layouts  1.3 us (2%)
    pallas_call x1, Pallas kernels, per_device(): pl.pallas_call(functools.partial(kernel, total_rows, scale), out_shape=ja...  70.8 us

profile of v3, /device:TPU:2, one launch (start us, length us, event | category | flops | bytes accessed | tf_op | source)
XLA Modules:
  0.0 72.1 jit_solution(5423635146363804157)
XLA Ops:
  0.0 70.8 %shard_map.37 = f32[16,128]{1,0:T(8,128)} custom-call(f32[2048,512]{1,0:T(8,128)} %bitcast.3, f32[64,512]{1,0:T(8,128)} %bitcast.4, f32[16]{0:T(128)} %damp_ref.1), custom_call_target="tpu_custom_call" | custom-call | tf_op jit(solution)/shard_map/pallas_call | solution.py:552
  70.8 1.3 %copy.5 = f32[128,16]{0,1:T(8,128)} copy(f32[128,16]{0,1:T(8,128)} %bitcast.5) | data formatting | bytes 16384

commit v4 on v3

--- a/solution.py
+++ b/solution.py
@@ -34,7 +34,8 @@
 SEC = EXC + 1
 FST = SEC + 6
 PAR = FST + 24
-ZED = PAR + 16
+PAR_LOW = PAR + 16
+ZED = PAR_LOW + 4
 COPIES = ZED + 8
 
 
@@ -428,7 +429,7 @@
     def far_first(b):
         for way in range(2):
             come(at(2, b, halves[way]), FST + 6 * b + 4 + way)
-        hand_over(2, b)
+            go(at(2, b, halves[way]), PAR_LOW + b if way else PAR + 8 + b, partner)
 
     def score(c, j):
         left = jnp.concatenate(split(cond[c, j]), axis=0)
@@ -443,7 +444,11 @@
     def other(a, b):
         c = 1 - core
         j = chip_at(wrap(snd + a), wrap(fst + b), c)
-        come(cond.at[c, j], PAR + a * 4 + b)
+        if a == 2:
+            come(cond.at[c, j, halves[0]], PAR + 8 + b)
+            come(cond.at[c, j, halves[1]], PAR_LOW + b)
+        else:
+            come(cond.at[c, j], PAR + a * 4 + b)
         score(c, j)
 
     acc[...] = jnp.zeros((2 * HALF_Q, ROWS), F32)
@@ -453,11 +458,11 @@
     for way in range(2):
         come(at(0, 3 - 2 * way, halves[way]), SEC + 2 * way)
         go(at(0, 3 - 2 * way, halves[way]), SEC + 4 + way, second_to[way])
+    pass_first(0)
     for way in range(2):
         come(at(0, 3 - 2 * way, halves[1 - way]), SEC + 2 * way + 1)
         along_first(3 - 2 * way)
         hand_over(0, 3 - 2 * way)
-    pass_first(0)
     rest_first(0)
     own(0, 0)
     for way in range(2):
@@ -510,32 +515,33 @@
         copy(zout.at[there], zin.at[i], ZED + i, (there, dp)).start()
         return carry
 
-    lax.fori_loop(1, DEPTH, send_scores, 0)
+    lax.fori_loop(DEPTH // 2, DEPTH, send_scores, 0)
+    lax.fori_loop(1, DEPTH // 2, send_scores, 0)
+    def sent_raw(k, carry):
+        copy(stage.at[0], rx.at[0], RAW + k, partner).wait_send()
+        return carry
+
+    lax.fori_loop(0, CHIPS, sent_raw, 0)
+
+    def sent_query(i, carry):
+        copy(qstage.at[0], qrx.at[0], QRY + i, partner).wait_send()
+        return carry
+
+    lax.fori_loop(1, CHIPS, sent_query, 0)
+
+    def sent_part(i, carry):
+        copy(part.at[0], r2.at[0], R1 + i, partner).wait_send()
+        return carry
+
+    lax.fori_loop(0, 12, sent_part, 0)
+    for c in (far_top, far_low, near_low, near_top, join_top, join_low, exchange, *sent):
+        c.wait_send()
+
     total = zout[z]
     for i in range(1, DEPTH):
         copy(zin.at[i], zin.at[i], ZED + i, partner).wait_recv()
         total = total + zin[i]
     out_ref[...] = jnp.concatenate([total[0:4], total[8:12], total[4:8], total[12:16]], axis=0)
-
-    def sent_raw(k, carry):
-        copy(stage.at[0], rx.at[0], RAW + k, partner).wait_send()
-        return carry
-
-    lax.fori_loop(0, CHIPS, sent_raw, 0)
-
-    def sent_query(i, carry):
-        copy(qstage.at[0], qrx.at[0], QRY + i, partner).wait_send()
-        return carry
-
-    lax.fori_loop(1, CHIPS, sent_query, 0)
-
-    def sent_part(i, carry):
-        copy(part.at[0], r2.at[0], R1 + i, partner).wait_send()
-        return carry
-
-    lax.fori_loop(0, 12, sent_part, 0)
-    for c in (far_top, far_low, near_low, near_top, join_top, join_low, exchange, *sent):
-        c.wait_send()
 
     def sent_scores(i, carry):
         copy(zout.at[0], zin.at[0], ZED + i, partner).wait_send()

time: 73.2 us -> 72.2 us (0.986)
  Pallas kernels: 70.8 us -> 69.7 us
    pallas_call x1, Pallas kernels: 70.8 us -> 69.7 us  [per_device(): pl.pallas_call(functools.partial(kernel, total_rows, scale), out_shape=ja...]
where the time goes in v4:
time: 72.2 us; the launch traced here: 71 us
  Pallas kernels  69.7 us (97%)
  local copies, waits for them, and re-layouts  1.3 us (2%)
    pallas_call x1, Pallas kernels, per_device(): pl.pallas_call(functools.partial(kernel, total_rows, scale), out_shape=ja...  69.7 us

profile of v4, /device:TPU:2, one launch (start us, length us, event | category | flops | bytes accessed | tf_op | source)
XLA Modules:
  0.0 71.0 jit_solution(8626263731795139530)
XLA Ops:
  0.0 69.7 %shard_map.37 = f32[16,128]{1,0:T(8,128)} custom-call(f32[2048,512]{1,0:T(8,128)} %bitcast.3, f32[64,512]{1,0:T(8,128)} %bitcast.4, f32[16]{0:T(128)} %damp_ref.1), custom_call_target="tpu_custom_call" | custom-call | tf_op jit(solution)/shard_map/pallas_call | solution.py:558
  69.7 1.3 %copy.5 = f32[128,16]{0,1:T(8,128)} copy(f32[128,16]{0,1:T(8,128)} %bitcast.5) | data formatting | bytes 16384

commit v5 on v4

--- a/solution.py
+++ b/solution.py
@@ -27,10 +27,10 @@
 RAW = 0
 QRY = RAW + 16
 R1 = QRY + 16
-R2 = R1 + 4
-R3 = R2 + 8
+R2 = R1 + 8
+R3 = R2 + 16
 R4 = R3 + 2
-EXC = R4 + 4
+EXC = R4 + 2
 SEC = EXC + 1
 FST = SEC + 6
 PAR = FST + 24
@@ -145,11 +145,9 @@
     def order(k):
         is0 = lax.div(CHIPS - 1 - k, 12)
         is3 = lax.div(k, 12)
-        i = (k - 4) * (1 - is0) * (1 - is3)
-        first = is0 * 2 + (1 - is0 - is3) * (1 + 2 * lax.rem(i, 2))
-        late = lax.div(i, 4)
-        middle = late * lax.div(i, 2) + (1 - late) * (1 - lax.rem(lax.div(i + 1, 2), 2))
-        b = (is0 + is3) * lax.rem(k, 4) + (1 - is0 - is3) * middle
+        near = 1 - is0 - is3
+        first = is0 * 2 + near * (1 + 2 * lax.rem(k, 2))
+        b = (is0 + is3) * lax.rem(k, 4) + near * lax.div(k - 4, 2)
         return first, b
 
     def module_of(k, c):
@@ -231,16 +229,6 @@
         part[k, 384:512, :] = first[:, 2 * LANES : 3 * LANES]
         part[k, 512:520, :] = jnp.broadcast_to(diagonal, (8, LANES))
 
-    def side(odd):
-        return 1 - 2 * odd
-
-    def far(i, carry):
-        gram(i)
-        copy(part.at[i], r1.at[i], R1 + i, dev(fst + side(lax.rem(i, 2)), snd)).start()
-        return carry
-
-    lax.fori_loop(0, 4, far, 0)
-
     def grams(low, high):
         def step(k, carry):
             gram(k)
@@ -248,30 +236,56 @@
 
         lax.fori_loop(low, high, step, 0)
 
-    def near(k, slot):
-        copy(part.at[k], r2.at[slot], R2 + slot, dev(fst + (1 if slot < 4 else -1), snd)).start()
-
-    def joined(k, i, slot):
-        copy(part.at[i], r1.at[i], R1 + i, partner).wait_recv()
-        part[k] = part[k] + r1[i]
-        near(k, slot)
-
-    grams(4, 5)
-    near(4, 1)
-    grams(5, 6)
-    near(5, 4)
-    grams(6, 12)
-    joined(6, 0, 0)
-    joined(7, 1, 5)
-    near(9, 6)
-    grams(12, 16)
-    joined(8, 2, 2)
-    near(10, 3)
-    joined(11, 3, 7)
+    halves = (pl.ds(0, TOP), pl.ds(TOP, TRI - TOP))
+    first_to = (dev(fst + 1, snd), dev(fst - 1, snd))
+
+    def ring(src, dst, h, place, way):
+        c = copy(src.at[halves[h]], dst.at[halves[h]], place, first_to[way])
+        c.start()
+        sent.append(c)
+
+    sent = []
+
+    def far(b):
+        for way in range(2):
+            ring(part.at[b], r1.at[b], way, R1 + 2 * b + way, way)
+
+    def near(b, way, h):
+        slot = 4 * way + b
+        ring(part.at[4 + 2 * b + way], r2.at[slot], h, R2 + 2 * slot + h, way)
+
+    def plain(b):
+        for way in range(2):
+            near(b, way, 1 - way)
+
+    def joined(b):
+        for way in range(2):
+            k, rows = 4 + 2 * b + way, halves[way]
+            copy(part.at[b, rows], r1.at[b, rows], R1 + 2 * b + way, partner).wait_recv()
+            part[k, rows] = part[k, rows] + r1[b, rows]
+            near(b, way, way)
+
+    for b in range(3):
+        grams(b, b + 1)
+        far(b)
+    grams(4, 6)
+    plain(0)
+    grams(3, 4)
+    grams(6, 10)
+    joined(0)
+    far(3)
+    plain(1)
+    grams(10, 16)
+    joined(1)
+    plain(2)
+    joined(2)
+    plain(3)
+    joined(3)
 
     def arrived(b):
-        for s in (0, 4):
-            copy(r2.at[s + b], r2.at[s + b], R2 + s + b, partner).wait_recv()
+        for slot in (b, 4 + b):
+            for h, rows in enumerate(halves):
+                copy(r2.at[slot, rows], r2.at[slot, rows], R2 + 2 * slot + h, partner).wait_recv()
         part[12 + b] = part[12 + b] + r2[b] + r2[4 + b]
 
     def wait_query(i, carry):
@@ -284,38 +298,22 @@
             [qrx[i, lb * 4 : lb * 4 + 4, :] for i in range(CHIPS)], axis=0
         )
 
-    top = pl.ds(0, TOP)
-    low = pl.ds(TOP, TRI - TOP)
-    plus = dev(fst, snd + 1)
-    minus = dev(fst, snd - 1)
-
-    def second_copy(b, rows, into, place, device):
-        return copy(part.at[12 + b, rows], into.at[rows], place, device)
-
+    second_to = (dev(fst, snd + 1), dev(fst, snd - 1))
     arrived(0)
-    far_top = second_copy(0, top, r3, R3, plus)
-    far_low = second_copy(0, low, r3, R3 + 1, minus)
-    far_top.start()
-    far_low.start()
-    arrived(1)
-    near_low = second_copy(1, low, r4.at[0], R4 + 1, plus)
-    near_low.start()
-    arrived(2)
-    near_top = second_copy(2, top, r4.at[1], R4 + 2, minus)
-    near_top.start()
-    far_top.wait_recv()
-    part[13, top] = part[13, top] + r3[top]
-    join_top = second_copy(1, top, r4.at[0], R4, plus)
-    join_top.start()
-    far_low.wait_recv()
-    part[14, low] = part[14, low] + r3[low]
-    join_low = second_copy(2, low, r4.at[1], R4 + 3, minus)
-    join_low.start()
+    over = []
+    for way, rows in enumerate(halves):
+        over.append(copy(part.at[12, rows], r3.at[rows], R3 + way, second_to[way]))
+        over[-1].start()
+    onto = []
+    for way, rows in enumerate(halves):
+        arrived(1 + way)
+        over[way].wait_recv()
+        part[13 + way, rows] = part[13 + way, rows] + r3[rows]
+        onto.append(copy(part.at[13 + way], r4.at[way], R4 + way, second_to[way]))
+        onto[-1].start()
     arrived(3)
-    near_low.wait_recv()
-    near_top.wait_recv()
-    join_top.wait_recv()
-    join_low.wait_recv()
+    for c in onto:
+        c.wait_recv()
     half[core] = (part[15] + r4[0] + r4[1]) * (1.0 / total_rows)
     exchange = copy(half.at[core], half.at[core], EXC, partner)
     exchange.start()
@@ -388,9 +386,6 @@
     cond[core, chip] = vector
 
     halves = (pl.ds(0, HALF_Q // 2), pl.ds(HALF_Q // 2, HALF_Q // 2))
-    first_to = (dev(fst + 1, snd), dev(fst - 1, snd))
-    second_to = (plus, minus)
-    sent = []
 
     def at(a, b, rows=None):
         ref = cond.at[core, chip_at(wrap(fst + a), wrap(snd + b))]
@@ -529,12 +524,7 @@
 
     lax.fori_loop(1, CHIPS, sent_query, 0)
 
-    def sent_part(i, carry):
-        copy(part.at[0], r2.at[0], R1 + i, partner).wait_send()
-        return carry
-
-    lax.fori_loop(0, 12, sent_part, 0)
-    for c in (far_top, far_low, near_low, near_top, join_top, join_low, exchange, *sent):
+    for c in (*over, *onto, exchange, *sent):
         c.wait_send()
 
     total = zout[z]

time: 72.2 us -> 71.5 us (level)
  no operation moved by 1% of the time
where the time goes in v5:
time: 71.5 us; the launch traced here: 70.5 us
  Pallas kernels  69.2 us (97%)
  local copies, waits for them, and re-layouts  1.3 us (2%)
    pallas_call x1, Pallas kernels, per_device(): pl.pallas_call(functools.partial(kernel, total_rows, scale), out_shape=ja...  69.2 us

profile of v5, /device:TPU:2, one launch (start us, length us, event | category | flops | bytes accessed | tf_op | source)
XLA Modules:
  0.0 70.5 jit_solution(13238579642540847326)
XLA Ops:
  0.0 69.2 %shard_map.37 = f32[16,128]{1,0:T(8,128)} custom-call(f32[2048,512]{1,0:T(8,128)} %bitcast.3, f32[64,512]{1,0:T(8,128)} %bitcast.4, f32[16]{0:T(128)} %damp_ref.1), custom_call_target="tpu_custom_call" | custom-call | tf_op jit(solution)/shard_map/pallas_call | solution.py:548
  69.2 1.3 %copy.5 = f32[128,16]{0,1:T(8,128)} copy(f32[128,16]{0,1:T(8,128)} %bitcast.5) | data formatting | bytes 16384

commit v6 on v5

--- a/solution.py
+++ b/solution.py
@@ -186,7 +186,6 @@
         stage_rows(k)
         return send_raw(k, carry)
 
-    lax.fori_loop(0, 4, send_raw, 0)
 
     def send_query(i, carry):
         there = lax.rem(chip + i, CHIPS)
@@ -194,6 +193,7 @@
         return carry
 
     lax.fori_loop(1, CHIPS, send_query, 0)
+    lax.fori_loop(0, 4, send_raw, 0)
     lax.fori_loop(4, CHIPS, stage_and_send, 0)
     qrx[chip] = qstage[chip]
 

time: 71.5 us -> 71.5 us (level)
  no operation moved by 1% of the time
where the time goes in v6:
time: 71.5 us; the launch traced here: 70.5 us
  Pallas kernels  69.2 us (97%)
  local copies, waits for them, and re-layouts  1.3 us (2%)
    pallas_call x1, Pallas kernels, per_device(): pl.pallas_call(functools.partial(kernel, total_rows, scale), out_shape=ja...  69.2 us

profile of v6, /device:TPU:2, one launch (start us, length us, event | category | flops | bytes accessed | tf_op | source)
XLA Modules:
  0.0 70.5 jit_solution(13980013601626985199)
XLA Ops:
  0.0 69.2 %shard_map.37 = f32[16,128]{1,0:T(8,128)} custom-call(f32[2048,512]{1,0:T(8,128)} %bitcast.3, f32[64,512]{1,0:T(8,128)} %bitcast.4, f32[16]{0:T(128)} %damp_ref.1), custom_call_target="tpu_custom_call" | custom-call | tf_op jit(solution)/shard_map/pallas_call | solution.py:548
  69.2 1.3 %copy.5 = f32[128,16]{0,1:T(8,128)} copy(f32[128,16]{0,1:T(8,128)} %bitcast.5) | data formatting | bytes 16384
